TPU v7x, 32 devices: a whole 2x2x4 slice. The times are simulated.
32 devices in a mesh: head: 8 (over z, y), ctx: 4 (over x, core).
Axes of the slice: x: 2, y: 2, z: 4, core: 2. Of those that a mesh axis runs over, the one named last changes fastest.
Arguments:
- queries: bfloat16 [64, 24576], P(('head', 'ctx')), may hold values from -5 to 5
- w_uk: bfloat16 [128, 128, 512], P('head'), may hold values from -0.5 to 0.5
- w_uv: bfloat16 [128, 512, 128], P('head'), may hold values from -0.25 to 0.25
- latent_cache: bfloat16 [512, 576], P('ctx'), may hold values from -8 to 8
- span_offset: int32 [1], replicated, may hold values from 0 to 448
Outputs:
- head_outputs: bfloat16 [64, 16384], P(('head', 'ctx'))
Inputs may be any that keep to these rules, and one draw needn't show every extreme that they name: The span's latents are in the cache at positions span_offset to span_offset + 63.
All inputs are finite; a program needn't handle non-finite values.
Results may differ from a plain program's by a relative error of at most 0.0071.
Values may be sent and summed in bfloat16 or wider, within the bound.
A program may use at most 64 MiB of HBM per device.

v0:
```python
import math

import jax
import jax.numpy as jnp
from jax import lax
from jax.sharding import PartitionSpec as P

NOPE = 128
ROPE = 64
LATENT = 512
VDIM = 128


yarn_mscale = 0.1 * math.log(40.0) + 1.0


def local(queries, w_uk, w_uv, latent_cache, span_offset):
    local_heads = w_uk.shape[0]
    query_width = NOPE + ROPE
    score_scale = query_width ** (-0.5) * yarn_mscale**2
    cycle_length = lax.axis_size("ctx")
    ctx_here = lax.axis_index("ctx")
    tokens_sent = queries.shape[0]
    regrouped = lax.all_to_all(queries, "head", split_axis=1, concat_axis=0, tiled=True)
    token_rows = regrouped.shape[0]
    shaped = regrouped.reshape(token_rows, local_heads, query_width)
    q_lat = jnp.einsum(
        "thn,hnl->thl", shaped[:, :, :NOPE], w_uk, preferred_element_type=jnp.float32
    ).astype(jnp.bfloat16)
    q_all = jnp.concatenate([q_lat, shaped[:, :, NOPE:]], axis=2).reshape(
        token_rows * local_heads, LATENT + ROPE
    )
    row_numbers = jnp.arange(token_rows, dtype=jnp.int32)
    token_index = (
        row_numbers // tokens_sent * cycle_length + ctx_here
    ) * tokens_sent + row_numbers % tokens_sent
    query_pos = jnp.repeat(span_offset[0] + token_index, local_heads)
    query_rows = token_rows * local_heads
    cache_piece = lax.all_gather(latent_cache, "ctx", axis=0, tiled=True)
    key_slots = jnp.arange(cache_piece.shape[0], dtype=jnp.int32)
    row_top = jnp.full((query_rows,), -1e30, jnp.float32)
    scores = (
        jnp.einsum("rc,kc->rk", q_all, cache_piece, preferred_element_type=jnp.float32)
        * score_scale
    )
    scores = jnp.where(key_slots[None, :] <= query_pos[:, None], scores, -jnp.inf)
    new_top = jnp.maximum(row_top, jnp.max(scores, axis=1))
    expo = jnp.exp(scores - new_top[:, None])
    row_total = jnp.sum(expo, axis=1)
    summed = jnp.dot(
        expo.astype(jnp.bfloat16), cache_piece[:, :LATENT], preferred_element_type=jnp.float32
    )
    final_state = (new_top, row_total, summed)
    row_top, row_total, summed = final_state
    attended = (
        (summed / row_total[:, None]).astype(jnp.bfloat16).reshape(token_rows, local_heads, LATENT)
    )
    projected = jnp.einsum(
        "thl,hlv->thv", attended, w_uv, preferred_element_type=jnp.float32
    ).astype(jnp.bfloat16)
    projected = projected.reshape(token_rows, local_heads * VDIM)
    return lax.all_to_all(projected, "head", split_axis=0, concat_axis=1, tiled=True)


def solution(mesh):
    return jax.shard_map(
        local,
        mesh=mesh,
        in_specs=(
            P(("head", "ctx"), None),
            P("head", None, None),
            P("head", None, None),
            P("ctx", None),
            P(),
        ),
        out_specs=P(("head", "ctx"), None),
        check_vma=False,
    )
```

profile of v0, /device:TPU:0, one launch (start us, length us, event | category | flops | bytes accessed | tf_op | source)
XLA Modules:
  0.0 32.6 jit_solution(17006953008275288717)
XLA Ops:
  0.0 0.0 copy-start
  0.0 7.4 %all-to-all-start = ((bf16[2,8,3072]{2,0,1:T(2,128)(2,1)}), bf16[2,8,3072]{2,0,1:T(2,128)(2,1)S(1)}, u32[]{:S(2)}, u32[]{:S(2)}) async-start(bf16[2,8,3072]{2,0,1:T(2,128)(2,1)} %bitcast.21), calls=%async_computation | async-start | bytes 196608 | tf_op jit(solution)/shard_map/all_to_all | solution.py:24
  8.1 0.1 broadcast_in_dim.13
  8.2 0.1 le.16
  8.2 7.7 %all_gather.3 = bf16[512,576]{0,1:T(8,128)(2,1)S(1)} all-gather(bf16[128,576]{0,1:T(8,128)(2,1)} %param.8), channel_id=1, replica_groups=mesh['head'=8,'ctx'=4] {'ctx'}, dimensions={0}, use_global_device_ids=true | all-gather | bytes 737280 | tf_op jit(solution)/shard_map/all_gather | solution.py:39
  16.0 0.0 all-to-all-done
  16.0 0.1 reshape.23
  16.2 0.0 copy-done
  16.2 0.4 %fusion.2 = bf16[16,16,512]{2,0,1:T(8,128)(2,1)S(1)} fusion(bf16[16,128,512]{2,1,0:T(8,128)(2,1)S(1)} %copy-done, bf16[16,16,128]{2,1,0:T(8,128)(2,1)S(1)} %slice.12), kind=kOutput, calls=%fused_computation.5 | convolution fusion | flops 33685504 | bytes 2424832 | tf_op jit(solution)/shard_map/thn,hnl->thl/dot_general | solution.py:27
  16.6 0.1 copy.10
  16.7 0.5 %fusion.16 = (f32[256]{0:T(256)S(1)}, f32[256,512]{1,0:T(8,128)S(1)}) fusion(bf16[256,576]{1,0:T(8,128)(2,1)S(1)} %bitcast.18, bf16[512,576]{0,1:T(8,128)(2,1)S(1)} %all_gather.3, s32[256]{0:T(256)S(1)} %le.16), kind=kOutput, calls=%fused_computation.28 | convolution fusion | flops 151518976 | bytes 1411072 | tf_op jit(solution)/shard_map/rc,kc->rk/dot_general | solution.py:43
  17.2 0.0 copy-start.1
  17.2 0.2 fusion.5
  17.4 0.4 %fusion.1 = bf16[256,512]{1,0:T(8,128)(2,1)S(1)} fusion(bf16[512,576]{0,1:T(8,128)(2,1)S(1)} %all_gather.3, f32[256,512]{1,0:T(8,128)S(1)} %get-tuple-element.6, f32[256]{0:T(256)S(1)} %fusion.5, f32[256]{0:T(256)S(1)} %broadcast_maximum_fusion), kind=kOutput, calls=%fused_computation.3 | convolution fusion | flops 134742016 | bytes 1312768 | tf_op jit(solution)/shard_map/dot_general | solution.py:50
  17.8 1.0 %copy-done.1 = bf16[16,512,128]{2,1,0:T(8,128)(2,1)S(1)} copy-done((bf16[16,512,128]{2,1,0:T(8,128)(2,1)S(1)}, bf16[16,512,128]{2,1,0:T(8,128)(2,1)}, u32[]{:S(2)}) %copy-start.1) | copy-done | bytes 2097176
  18.8 0.5 %fusion.3 = bf16[16,16,128]{2,0,1:T(8,128)(2,1)S(1)} fusion(bf16[16,512,128]{2,1,0:T(8,128)(2,1)S(1)} %copy-done.1, bf16[16,16,512]{2,1,0:T(8,128)(2,1)S(1)} %bitcast.19), kind=kOutput, calls=%fused_computation.7 | convolution fusion | flops 33587200 | bytes 2424832 | tf_op jit(solution)/shard_map/thl,hlv->thv/dot_general | solution.py:58
  19.3 12.7 %all_to_all.35 = bf16[8,2,2048]{2,1,0:T(2,128)(2,1)S(1)} all-to-all(bf16[8,2,2048]{2,1,0:T(2,128)(2,1)S(1)} %all_to_all.29), channel_id=1, replica_groups=mesh['head'=8,'ctx'=4] {'head'}, dimensions={0} | all-to-all | bytes 131072 | tf_op jit(solution)/shard_map/all_to_all | solution.py:62
  32.0 0.6 %copy.21 = bf16[2,16384]{1,0:T(2,128)(2,1)} copy(bf16[2,16384]{1,0:T(2,128)(2,1)S(1)} %bitcast.20) | data formatting | bytes 131072
  (8 shorter events, 0.2 us)
Async XLA Ops:
  0.0 16.2 %copy-start = (bf16[16,128,512]{2,1,0:T(8,128)(2,1)S(1)}, bf16[16,128,512]{2,1,0:T(8,128)(2,1)}, u32[]{:S(2)}) copy-start(bf16[16,128,512]{2,1,0:T(8,128)(2,1)} %param.6) | copy-start | bytes 6291460
  0.0 16.0 %all-to-all-start = ((bf16[2,8,3072]{2,0,1:T(2,128)(2,1)}), bf16[2,8,3072]{2,0,1:T(2,128)(2,1)S(1)}, u32[]{:S(2)}, u32[]{:S(2)}) async-start(bf16[2,8,3072]{2,0,1:T(2,128)(2,1)} %bitcast.21), calls=%async_computation | async-start | bytes 196608 | tf_op jit(solution)/shard_map/all_to_all | solution.py:24
  17.2 1.6 %copy-start.1 = (bf16[16,512,128]{2,1,0:T(8,128)(2,1)S(1)}, bf16[16,512,128]{2,1,0:T(8,128)(2,1)}, u32[]{:S(2)}) copy-start(bf16[16,512,128]{2,1,0:T(8,128)(2,1)} %param.7) | copy-start | bytes 6291460
where the time goes:
time: 32.9 us; the launch traced here: 32.6 us
  blocking collectives  20.4 us (62%)
  starting transfers between devices  7.41 us (23%)
  local copies, waits for them, and re-layouts  2.06 us (6%)
  matrix products  1.67 us (5%)
  between operations  0.75 us (2%)
    all_to_all x1, blocking collectives, local(): lax.all_to_all(projected, 'head', split_axis=0, concat_axis=1, tiled=True)  12.7 us
    all_gather x1, blocking collectives, local(): cache_piece = lax.all_gather(latent_cache, 'ctx', axis=0, tiled=True)  7.74 us
    all_to_all x1, starting transfers between devices, local(): lax.all_to_all(queries, 'head', split_axis=1, concat_axis=0, tiled=True)  7.41 us
    unnamed x6, local copies, waits for them, and re-layouts  1.64 us
  transfers between devices with their start and end apart: 1, of which 0 were waited for; matrix products, arithmetic and copies ran while one was open for 0% of the time, Pallas kernels for 0%

commit v1 on v0

v1 whole, which is shorter than its diff:
```python
import functools
import math

import jax
import jax.numpy as jnp
from jax import lax
from jax.experimental import pallas as pl
from jax.experimental.pallas import tpu as pltpu
from jax.sharding import PartitionSpec as P

NOPE = 128
ROPE = 64
LATENT = 512
VDIM = 128
WIDTH = NOPE + ROPE
MESH = pl.DeviceIdType.MESH

yarn_mscale = 0.1 * math.log(40.0) + 1.0
score_scale = WIDTH ** (-0.5) * yarn_mscale**2


def kernel(
    n_head, n_ctx, q_hbm, uk_hbm, uv_hbm, cache_hbm, offset_ref, out_ref,
    q_in, q_got, q_rows, uk, uv, q_all, cache, scores, acc, heads_out, slabs,
    local_sem, q_send, q_recv, own_send, fwd_send, cache_recv, o_send, o_recv,
):
    tokens = q_hbm.shape[0]
    heads = uk_hbm.shape[0]
    span = cache_hbm.shape[0]
    chips = n_ctx // 2
    all_tokens = n_head * tokens
    rows = heads * all_tokens
    q_cols = heads * WIDTH
    o_cols = heads * VDIM
    h_me = lax.axis_index("head")
    c_me = lax.axis_index("ctx")
    chip = c_me // 2
    core = c_me % 2
    sibling = chip * 2 + 1 - core

    def head_peer(i):
        return lax.rem(h_me + i, n_head)

    def chip_peer(i):
        return lax.rem(chip + i, chips)

    def piece(chip_at, core_at):
        return cache.at[chip_at, pl.ds(pl.multiple_of(core_at * span, span), span), :]

    load_q = pltpu.make_async_copy(q_hbm, q_in, local_sem.at[0])
    load_cache = pltpu.make_async_copy(cache_hbm, piece(chip, core), local_sem.at[1])
    load_uk = pltpu.make_async_copy(uk_hbm, uk, local_sem.at[2])
    load_uv = pltpu.make_async_copy(uv_hbm, uv, local_sem.at[3])
    load_q.start()
    load_cache.start()
    load_uk.start()
    load_uv.start()

    barrier = pltpu.get_barrier_semaphore()
    for i in range(1, n_head):
        pl.semaphore_signal(barrier, inc=1, device_id=(head_peer(i), c_me), device_id_type=MESH)
    for i in range(1, chips):
        pl.semaphore_signal(
            barrier, inc=1, device_id=(h_me, chip_peer(i) * 2 + core), device_id_type=MESH
        )
    pl.semaphore_signal(barrier, inc=1, device_id=(h_me, sibling), device_id_type=MESH)
    load_q.wait()
    load_cache.wait()
    pl.semaphore_wait(barrier, n_head - 1 + chips)

    cache_far = []
    for i in range(1, chips):
        there = chip_peer(i)
        copy = pltpu.make_async_remote_copy(
            src_ref=piece(chip, core),
            dst_ref=piece(chip, core),
            send_sem=own_send.at[i],
            recv_sem=cache_recv.at[chip, core],
            device_id=(h_me, there * 2 + core),
            device_id_type=MESH,
        )
        copy.start()
        cache_far.append(copy)
    q_copies = []
    for i in range(1, n_head):
        there = head_peer(i)
        copy = pltpu.make_async_remote_copy(
            src_ref=q_in.at[:, pl.ds(pl.multiple_of(there * q_cols, 128), q_cols)],
            dst_ref=q_got.at[h_me],
            send_sem=q_send.at[i],
            recv_sem=q_recv.at[h_me],
            device_id=(there, c_me),
            device_id_type=MESH,
        )
        copy.start()
        q_copies.append(copy)
    to_sibling = pltpu.make_async_remote_copy(
        src_ref=piece(chip, core),
        dst_ref=piece(chip, core),
        send_sem=own_send.at[0],
        recv_sem=cache_recv.at[chip, core],
        device_id=(h_me, sibling),
        device_id_type=MESH,
    )
    to_sibling.start()
    own_q = pltpu.make_async_copy(
        q_in.at[:, pl.ds(pl.multiple_of(h_me * q_cols, 128), q_cols)],
        q_got.at[h_me],
        local_sem.at[4],
    )
    own_q.start()
    own_q.wait()

    def arrival(sem, dst, src=None):
        return pltpu.make_async_remote_copy(
            src_ref=dst,
            dst_ref=dst,
            send_sem=sem,
            recv_sem=sem,
            device_id=(h_me, sibling),
            device_id_type=MESH,
        )

    for i in range(1, n_head):
        there = head_peer(i)
        arrival(q_recv.at[there], q_got.at[there]).wait_recv()
    for p in range(n_head):
        q_rows[p * tokens : (p + 1) * tokens, :] = q_got[p].astype(jnp.float32)
    load_uk.wait()
    for pair in range(heads // 2):
        both = q_rows[:, pair * 2 * WIDTH : (pair + 1) * 2 * WIDTH].astype(jnp.bfloat16)
        for k in range(2):
            h = pair * 2 + k
            at = pl.ds(h * all_tokens, all_tokens)
            plain = both[:, k * WIDTH : k * WIDTH + NOPE]
            turned = both[:, k * WIDTH + NOPE : (k + 1) * WIDTH]
            q_all[at, :LATENT] = jnp.dot(
                plain, uk[h], preferred_element_type=jnp.float32
            ).astype(jnp.bfloat16)
            q_all[at, LATENT:] = turned

    forwards = []
    for i in range(1, chips):
        there = chip_peer(i)
        arrival(cache_recv.at[there, core], piece(there, core)).wait_recv()
        copy = pltpu.make_async_remote_copy(
            src_ref=piece(there, core),
            dst_ref=piece(there, core),
            send_sem=fwd_send.at[i],
            recv_sem=cache_recv.at[there, core],
            device_id=(h_me, sibling),
            device_id_type=MESH,
        )
        copy.start()
        forwards.append(copy)

    row = lax.broadcasted_iota(jnp.int32, (rows, 1), 0)
    token = lax.rem(row, all_tokens)
    token = (lax.div(token, tokens) * n_ctx + c_me) * tokens + lax.rem(token, tokens)
    query_pos = token + offset_ref[0]
    lane = lax.broadcasted_iota(jnp.int32, (rows, 2 * span), 1)

    def score_step(i, top):
        at = chip_peer(i)
        arrival(cache_recv.at[at, 1 - core], piece(at, 1 - core)).wait_recv()
        s = (
            lax.dot_general(
                q_all[...],
                cache[at],
                (((1,), (1,)), ((), ())),
                preferred_element_type=jnp.float32,
            )
            * score_scale
        )
        s = jnp.where(lane + at * (2 * span) <= query_pos, s, -jnp.inf)
        scores[at] = s
        return jnp.maximum(top, jnp.max(s, axis=1, keepdims=True))

    unroll = chips if chips <= 4 else 1
    top = lax.fori_loop(
        0, chips, score_step, jnp.full((rows, 1), -jnp.inf, jnp.float32), unroll=unroll
    )
    acc[...] = jnp.zeros_like(acc)

    def value_step(i, total):
        at = chip_peer(i)
        expo = jnp.exp(scores[at] - top)
        acc[...] += jnp.dot(
            expo.astype(jnp.bfloat16), cache[at, :, :LATENT], preferred_element_type=jnp.float32
        )
        return total + jnp.sum(expo, axis=1, keepdims=True)

    total = lax.fori_loop(
        0, chips, value_step, jnp.zeros((rows, 1), jnp.float32), unroll=unroll
    )
    attended = (acc[...] / total).astype(jnp.bfloat16)
    load_uv.wait()
    for h in range(heads):
        heads_out[:, h * VDIM : (h + 1) * VDIM] = jnp.dot(
            attended[h * all_tokens : (h + 1) * all_tokens],
            uv[h],
            preferred_element_type=jnp.float32,
        )
    for p in range(n_head):
        slabs[p] = heads_out[p * tokens : (p + 1) * tokens, :].astype(jnp.bfloat16)

    mine = pl.ds(pl.multiple_of(h_me * o_cols, 128), o_cols)
    out_copies = []
    for i in range(1, n_head):
        there = head_peer(i)
        copy = pltpu.make_async_remote_copy(
            src_ref=slabs.at[there],
            dst_ref=out_ref.at[:, mine],
            send_sem=o_send.at[i],
            recv_sem=o_recv.at[h_me],
            device_id=(there, c_me),
            device_id_type=MESH,
        )
        copy.start()
        out_copies.append(copy)
    own_out = pltpu.make_async_copy(slabs.at[h_me], out_ref.at[:, mine], local_sem.at[5])
    own_out.start()

    for copy in cache_far + q_copies + [to_sibling] + forwards:
        copy.wait_send()
    own_out.wait()
    for i in range(1, n_head):
        there = head_peer(i)
        cols = pl.ds(pl.multiple_of(there * o_cols, 128), o_cols)
        arrival(o_recv.at[there], out_ref.at[:, cols]).wait_recv()
    for copy in out_copies:
        copy.wait_send()


def local(n_head, n_ctx, queries, w_uk, w_uv, latent_cache, span_offset):
    tokens = queries.shape[0]
    heads = w_uk.shape[0]
    span = latent_cache.shape[0]
    chips = n_ctx // 2
    all_tokens = n_head * tokens
    rows = heads * all_tokens
    bf16, f32 = jnp.bfloat16, jnp.float32
    dma = pltpu.SemaphoreType.DMA
    anywhere = pl.BlockSpec(memory_space=pl.ANY)
    return pl.pallas_call(
        functools.partial(kernel, n_head, n_ctx),
        out_shape=jax.ShapeDtypeStruct((tokens, n_head * heads * VDIM), bf16),
        in_specs=[anywhere] * 4 + [pl.BlockSpec(memory_space=pltpu.SMEM)],
        out_specs=pl.BlockSpec(memory_space=pltpu.VMEM),
        scratch_shapes=[
            pltpu.VMEM(queries.shape, bf16),
            pltpu.VMEM((n_head, tokens, heads * WIDTH), bf16),
            pltpu.VMEM((all_tokens, heads * WIDTH), f32),
            pltpu.VMEM(w_uk.shape, bf16),
            pltpu.VMEM(w_uv.shape, bf16),
            pltpu.VMEM((rows, LATENT + ROPE), bf16),
            pltpu.VMEM((chips, 2 * span, LATENT + ROPE), bf16),
            pltpu.VMEM((chips, rows, 2 * span), f32),
            pltpu.VMEM((rows, LATENT), f32),
            pltpu.VMEM((all_tokens, heads * VDIM), f32),
            pltpu.VMEM((n_head, tokens, heads * VDIM), bf16),
            dma((6,)),
            dma((n_head,)),
            dma((n_head,)),
            dma((chips,)),
            dma((chips,)),
            dma((chips, 2)),
            dma((n_head,)),
            dma((n_head,)),
        ],
        compiler_params=pltpu.CompilerParams(
            collective_id=0, has_side_effects=True, vmem_limit_bytes=40 * 1024 * 1024
        ),
    )(queries, w_uk, w_uv, latent_cache, span_offset)


def solution(mesh):
    return jax.shard_map(
        functools.partial(local, mesh.shape["head"], mesh.shape["ctx"]),
        mesh=mesh,
        in_specs=(
            P(("head", "ctx"), None),
            P("head", None, None),
            P("head", None, None),
            P("ctx", None),
            P(),
        ),
        out_specs=P(("head", "ctx"), None),
        check_vma=False,
    )
```

time: 32.9 us -> 24.5 us (0.74)
  blocking collectives: 20.4 us -> 0 us
  Pallas kernels: 0 us -> 17.8 us
  starting transfers between devices: 7.41 us -> 0 us
  local copies, waits for them, and re-layouts: 2.06 us -> 5.76 us
  matrix products: 1.67 us -> 0 us
    pallas_call x0 -> x1, Pallas kernels: none -> 17.8 us  [local(): pl.pallas_call(functools.partial(kernel, n_head, n_ctx), out_shape=jax.Sh...]
    all_to_all x1 -> x0, blocking collectives: 12.7 us -> none  [local(): lax.all_to_all(projected, 'head', split_axis=0, concat_axis=1, tiled=True)]
    all_gather x1 -> x0, blocking collectives: 7.74 us -> none  [local(): cache_piece = lax.all_gather(latent_cache, 'ctx', axis=0, tiled=True)]
    all_to_all x1 -> x0, starting transfers between devices: 7.41 us -> none  [local(): lax.all_to_all(queries, 'head', split_axis=1, concat_axis=0, tiled=True)]
    unnamed x6 -> x8, local copies, waits for them, and re-layouts: 1.64 us -> 5.76 us
    dot_general x4 -> x0, matrix products: 1.67 us -> none  [the longest x1 0.47 us: local(): jnp.einsum('thl,hlv->thv', attended, w_uv, preferred_element_type=jnp.flo...]
  transfers between devices with their start and end apart: 1 -> 0, of which waited for: 0 -> 0; matrix products, arithmetic and copies ran while one was open for 0% -> 0% of each run, Pallas kernels for 0% -> 0%
where the time goes in v1:
time: 24.5 us; the launch traced here: 24.2 us
  Pallas kernels  17.8 us (73%)
  local copies, waits for them, and re-layouts  5.76 us (24%)
  between operations  0.67 us (3%)
    pallas_call x1, Pallas kernels, local(): pl.pallas_call(functools.partial(kernel, n_head, n_ctx), out_shape=jax.Sh...  17.8 us
    unnamed x8, local copies, waits for them, and re-layouts  5.76 us

profile of v1, /device:TPU:0, one launch (start us, length us, event | category | flops | bytes accessed | tf_op | source)
XLA Modules:
  0.0 24.2 jit_solution(10623637571348680301)
XLA Ops:
  0.7 1.1 %copy.6.cache_hbm = bf16[128,576]{1,0:T(8,128)(2,1)S(1)} copy(bf16[128,576]{0,1:T(8,128)(2,1)} %param.8) | data formatting | bytes 294912 | tf_op args[3]
  1.7 0.0 copy-start
  1.7 1.6 %copy-done = bf16[16,128,512]{2,1,0:T(8,128)(2,1)S(1)} copy-done((bf16[16,128,512]{2,1,0:T(8,128)(2,1)S(1)}, bf16[16,128,512]{2,1,0:T(8,128)(2,1)}, u32[]{:S(2)}) %copy-start) | copy-done | bytes 2097176
  3.3 0.0 copy-start.1
  3.3 1.6 %copy-done.1 = bf16[16,512,128]{2,1,0:T(8,128)(2,1)S(1)} copy-done((bf16[16,512,128]{2,1,0:T(8,128)(2,1)S(1)}, bf16[16,512,128]{2,1,0:T(8,128)(2,1)}, u32[]{:S(2)}) %copy-start.1) | copy-done | bytes 2097176
  4.9 0.0 copy-start.2
  4.9 0.9 %copy-done.2 = bf16[2,24576]{1,0:T(2,128)(2,1)S(1)} copy-done((bf16[2,24576]{1,0:T(2,128)(2,1)S(1)}, bf16[2,24576]{1,0:T(2,128)(2,1)}, u32[]{:S(2)}) %copy-start.2) | copy-done | bytes 98328
  5.8 17.8 %shard_map.55 = bf16[2,16384]{1,0:T(2,128)(2,1)S(1)} custom-call(bf16[2,24576]{1,0:T(2,128)(2,1)S(1)} %copy-done.2, bf16[16,128,512]{2,1,0:T(8,128)(2,1)S(1)} %copy-done, bf16[16,512,128]{2,1,0:T(8,128)(2,1)S(1)} %copy-done.1, bf16[128,576]{1,0:T(8,128)(2,1)S(1)} %copy.6.cache_hbm, s32[1]{0:T(128)S(6)} %copy.8.offset_ref), custom_call_target="tpu_custom_call" | custom-call | tf_op jit(solution)/shard_map/pallas_call | solution.py:245
  23.6 0.6 %copy.9 = bf16[2,16384]{1,0:T(2,128)(2,1)} copy(bf16[2,16384]{1,0:T(2,128)(2,1)S(1)} %shard_map.55) | data formatting | bytes 131072
Async XLA Ops:
  1.7 1.6 %copy-start = (bf16[16,128,512]{2,1,0:T(8,128)(2,1)S(1)}, bf16[16,128,512]{2,1,0:T(8,128)(2,1)}, u32[]{:S(2)}) copy-start(bf16[16,128,512]{2,1,0:T(8,128)(2,1)} %uk_hbm.1) | copy-start | bytes 6291460
  3.3 1.6 %copy-start.1 = (bf16[16,512,128]{2,1,0:T(8,128)(2,1)S(1)}, bf16[16,512,128]{2,1,0:T(8,128)(2,1)}, u32[]{:S(2)}) copy-start(bf16[16,512,128]{2,1,0:T(8,128)(2,1)} %uv_hbm.1) | copy-start | bytes 6291460
  4.9 0.9 %copy-start.2 = (bf16[2,24576]{1,0:T(2,128)(2,1)S(1)}, bf16[2,24576]{1,0:T(2,128)(2,1)}, u32[]{:S(2)}) copy-start(bf16[2,24576]{1,0:T(2,128)(2,1)} %q_hbm.1) | copy-start | bytes 294916

commit v2 on v1

--- a/solution.py
+++ b/solution.py
@@ -26,7 +26,7 @@
 ):
     tokens = q_hbm.shape[0]
     heads = uk_hbm.shape[0]
-    span = cache_hbm.shape[0]
+    span = cache_hbm.shape[1]
     chips = n_ctx // 2
     all_tokens = n_head * tokens
     rows = heads * all_tokens
@@ -45,7 +45,7 @@
         return lax.rem(chip + i, chips)
 
     def piece(chip_at, core_at):
-        return cache.at[chip_at, pl.ds(pl.multiple_of(core_at * span, span), span), :]
+        return cache.at[chip_at, core_at]
 
     load_q = pltpu.make_async_copy(q_hbm, q_in, local_sem.at[0])
     load_cache = pltpu.make_async_copy(cache_hbm, piece(chip, core), local_sem.at[1])
@@ -163,15 +163,8 @@
     def score_step(i, top):
         at = chip_peer(i)
         arrival(cache_recv.at[at, 1 - core], piece(at, 1 - core)).wait_recv()
-        s = (
-            lax.dot_general(
-                q_all[...],
-                cache[at],
-                (((1,), (1,)), ((), ())),
-                preferred_element_type=jnp.float32,
-            )
-            * score_scale
-        )
+        keys = jnp.concatenate([cache[at, 0], cache[at, 1]], axis=1)
+        s = jnp.dot(q_all[...], keys, preferred_element_type=jnp.float32) * score_scale
         s = jnp.where(lane + at * (2 * span) <= query_pos, s, -jnp.inf)
         scores[at] = s
         return jnp.maximum(top, jnp.max(s, axis=1, keepdims=True))
@@ -185,8 +178,12 @@
     def value_step(i, total):
         at = chip_peer(i)
         expo = jnp.exp(scores[at] - top)
-        acc[...] += jnp.dot(
-            expo.astype(jnp.bfloat16), cache[at, :, :LATENT], preferred_element_type=jnp.float32
+        values = jnp.concatenate([cache[at, 0, :LATENT], cache[at, 1, :LATENT]], axis=1)
+        acc[...] += lax.dot_general(
+            expo.astype(jnp.bfloat16),
+            values,
+            (((1,), (1,)), ((), ())),
+            preferred_element_type=jnp.float32,
         )
         return total + jnp.sum(expo, axis=1, keepdims=True)
 
@@ -241,7 +238,7 @@
     rows = heads * all_tokens
     bf16, f32 = jnp.bfloat16, jnp.float32
     dma = pltpu.SemaphoreType.DMA
-    anywhere = pl.BlockSpec(memory_space=pl.ANY)
+    anywhere = pl.BlockSpec(memory_space=pltpu.HBM)
     return pl.pallas_call(
         functools.partial(kernel, n_head, n_ctx),
         out_shape=jax.ShapeDtypeStruct((tokens, n_head * heads * VDIM), bf16),
@@ -254,7 +251,7 @@
             pltpu.VMEM(w_uk.shape, bf16),
             pltpu.VMEM(w_uv.shape, bf16),
             pltpu.VMEM((rows, LATENT + ROPE), bf16),
-            pltpu.VMEM((chips, 2 * span, LATENT + ROPE), bf16),
+            pltpu.VMEM((chips, 2, LATENT + ROPE, span), bf16),
             pltpu.VMEM((chips, rows, 2 * span), f32),
             pltpu.VMEM((rows, LATENT), f32),
             pltpu.VMEM((all_tokens, heads * VDIM), f32),
@@ -269,9 +266,9 @@
             dma((n_head,)),
         ],
         compiler_params=pltpu.CompilerParams(
-            collective_id=0, has_side_effects=True, vmem_limit_bytes=40 * 1024 * 1024
+            collective_id=0, has_side_effects=True, vmem_limit_bytes=64 * 1024 * 1024 - 64 * 1024
         ),
-    )(queries, w_uk, w_uv, latent_cache, span_offset)
+    )(queries, w_uk, w_uv, latent_cache.T, span_offset)
 
 
 def solution(mesh):

time: 24.5 us -> 20.1 us (0.82)
  local copies, waits for them, and re-layouts: 5.76 us -> 1.52 us
    unnamed x8 -> x1, local copies, waits for them, and re-layouts: 5.76 us -> 1.52 us
where the time goes in v2:
time: 20.1 us; the launch traced here: 20 us
  Pallas kernels  17.8 us (89%)
  local copies, waits for them, and re-layouts  1.52 us (8%)
  between operations  0.66 us (3%)
    pallas_call x1, Pallas kernels, local(): pl.pallas_call(functools.partial(kernel, n_head, n_ctx), out_shape=jax.Sh...  17.8 us
    unnamed x1, local copies, waits for them, and re-layouts  1.52 us

profile of v2, /device:TPU:0, one launch (start us, length us, event | category | flops | bytes accessed | tf_op | source)
XLA Modules:
  0.0 20.0 jit_solution(6698404760715957741)
XLA Ops:
  0.7 17.8 %shard_map.55 = bf16[2,16384]{1,0:T(2,128)(2,1)} custom-call(bf16[2,24576]{1,0:T(2,128)(2,1)} %q_hbm.1, bf16[16,128,512]{2,1,0:T(8,128)(2,1)} %uk_hbm.1, bf16[16,512,128]{2,1,0:T(8,128)(2,1)} %uv_hbm.1, bf16[576,128]{1,0:T(8,128)(2,1)} %bitcast.1, s32[1]{0:T(128)S(6)} %copy.7.offset_ref), custom_call_target="tpu_custom_call" | custom-call | tf_op jit(solution)/shard_map/pallas_call | solution.py:242
  18.4 1.5 %copy.8 = bf16[2,16384]{1,0:T(2,128)(2,1)} copy(bf16[2,16384]{1,0:T(2,128)(2,1)} %shard_map.55) | data formatting | bytes 131072

commit v3 on v2

--- a/solution.py
+++ b/solution.py
@@ -154,77 +154,96 @@
         copy.start()
         forwards.append(copy)
 
-    row = lax.broadcasted_iota(jnp.int32, (rows, 1), 0)
+    parts = slabs.shape[0]
+    row = lax.broadcasted_iota(jnp.int32, (rows // parts, 1), 0)
     token = lax.rem(row, all_tokens)
     token = (lax.div(token, tokens) * n_ctx + c_me) * tokens + lax.rem(token, tokens)
     query_pos = token + offset_ref[0]
-    lane = lax.broadcasted_iota(jnp.int32, (rows, 2 * span), 1)
-
-    def score_step(i, top):
+    lane = lax.broadcasted_iota(jnp.int32, (rows // parts, 2 * span), 1)
+
+    for i in range(chips):
         at = chip_peer(i)
         arrival(cache_recv.at[at, 1 - core], piece(at, 1 - core)).wait_recv()
-        keys = jnp.concatenate([cache[at, 0], cache[at, 1]], axis=1)
-        s = jnp.dot(q_all[...], keys, preferred_element_type=jnp.float32) * score_scale
-        s = jnp.where(lane + at * (2 * span) <= query_pos, s, -jnp.inf)
-        scores[at] = s
-        return jnp.maximum(top, jnp.max(s, axis=1, keepdims=True))
 
     unroll = chips if chips <= 4 else 1
-    top = lax.fori_loop(
-        0, chips, score_step, jnp.full((rows, 1), -jnp.inf, jnp.float32), unroll=unroll
-    )
-    acc[...] = jnp.zeros_like(acc)
-
-    def value_step(i, total):
-        at = chip_peer(i)
-        expo = jnp.exp(scores[at] - top)
-        values = jnp.concatenate([cache[at, 0, :LATENT], cache[at, 1, :LATENT]], axis=1)
-        acc[...] += lax.dot_general(
-            expo.astype(jnp.bfloat16),
-            values,
-            (((1,), (1,)), ((), ())),
-            preferred_element_type=jnp.float32,
-        )
-        return total + jnp.sum(expo, axis=1, keepdims=True)
-
-    total = lax.fori_loop(
-        0, chips, value_step, jnp.zeros((rows, 1), jnp.float32), unroll=unroll
-    )
-    attended = (acc[...] / total).astype(jnp.bfloat16)
-    load_uv.wait()
-    for h in range(heads):
-        heads_out[:, h * VDIM : (h + 1) * VDIM] = jnp.dot(
-            attended[h * all_tokens : (h + 1) * all_tokens],
-            uv[h],
-            preferred_element_type=jnp.float32,
-        )
-    for p in range(n_head):
-        slabs[p] = heads_out[p * tokens : (p + 1) * tokens, :].astype(jnp.bfloat16)
-
-    mine = pl.ds(pl.multiple_of(h_me * o_cols, 128), o_cols)
+    part_heads = heads // parts
+    part_rows = rows // parts
+    part_cols = part_heads * VDIM
     out_copies = []
-    for i in range(1, n_head):
-        there = head_peer(i)
-        copy = pltpu.make_async_remote_copy(
-            src_ref=slabs.at[there],
-            dst_ref=out_ref.at[:, mine],
-            send_sem=o_send.at[i],
-            recv_sem=o_recv.at[h_me],
-            device_id=(there, c_me),
-            device_id_type=MESH,
-        )
-        copy.start()
-        out_copies.append(copy)
-    own_out = pltpu.make_async_copy(slabs.at[h_me], out_ref.at[:, mine], local_sem.at[5])
-    own_out.start()
+    own_outs = []
+    for part in range(parts):
+        here = slice(part * part_rows, (part + 1) * part_rows)
+
+        def score_step(i, top):
+            at = chip_peer(i)
+            keys = jnp.concatenate([cache[at, 0], cache[at, 1]], axis=1)
+            s = jnp.dot(q_all[here], keys, preferred_element_type=jnp.float32) * score_scale
+            s = jnp.where(lane + at * (2 * span) <= query_pos, s, -jnp.inf)
+            scores[at, here] = s
+            return jnp.maximum(top, jnp.max(s, axis=1, keepdims=True))
+
+        top = lax.fori_loop(
+            0, chips, score_step, jnp.full((part_rows, 1), -jnp.inf, jnp.float32), unroll=unroll
+        )
+        acc[here] = jnp.zeros((part_rows, LATENT), jnp.float32)
+
+        def value_step(i, total):
+            at = chip_peer(i)
+            expo = jnp.exp(scores[at, here] - top)
+            values = jnp.concatenate([cache[at, 0, :LATENT], cache[at, 1, :LATENT]], axis=1)
+            acc[here] += lax.dot_general(
+                expo.astype(jnp.bfloat16),
+                values,
+                (((1,), (1,)), ((), ())),
+                preferred_element_type=jnp.float32,
+            )
+            return total + jnp.sum(expo, axis=1, keepdims=True)
+
+        total = lax.fori_loop(
+            0, chips, value_step, jnp.zeros((part_rows, 1), jnp.float32), unroll=unroll
+        )
+        attended = (acc[here] / total).astype(jnp.bfloat16)
+        if part == 0:
+            load_uv.wait()
+        for k in range(part_heads):
+            h = part * part_heads + k
+            heads_out[:, h * VDIM : (h + 1) * VDIM] = jnp.dot(
+                attended[k * all_tokens : (k + 1) * all_tokens],
+                uv[h],
+                preferred_element_type=jnp.float32,
+            )
+        cols = slice(part * part_cols, (part + 1) * part_cols)
+        for p in range(n_head):
+            slabs[part, p] = heads_out[p * tokens : (p + 1) * tokens, cols].astype(jnp.bfloat16)
+        start = pl.multiple_of(h_me * o_cols + part * part_cols, 128)
+        mine = pl.ds(start, part_cols)
+        for i in range(1, n_head):
+            there = head_peer(i)
+            copy = pltpu.make_async_remote_copy(
+                src_ref=slabs.at[part, there],
+                dst_ref=out_ref.at[:, mine],
+                send_sem=o_send.at[part, i],
+                recv_sem=o_recv.at[part, h_me],
+                device_id=(there, c_me),
+                device_id_type=MESH,
+            )
+            copy.start()
+            out_copies.append(copy)
+        own_out = pltpu.make_async_copy(
+            slabs.at[part, h_me], out_ref.at[:, mine], local_sem.at[5 + part]
+        )
+        own_out.start()
+        own_outs.append(own_out)
 
     for copy in cache_far + q_copies + [to_sibling] + forwards:
         copy.wait_send()
-    own_out.wait()
-    for i in range(1, n_head):
-        there = head_peer(i)
-        cols = pl.ds(pl.multiple_of(there * o_cols, 128), o_cols)
-        arrival(o_recv.at[there], out_ref.at[:, cols]).wait_recv()
+    for own_out in own_outs:
+        own_out.wait()
+    for part in range(parts):
+        for i in range(1, n_head):
+            there = head_peer(i)
+            start = pl.multiple_of(there * o_cols + part * part_cols, 128)
+            arrival(o_recv.at[part, there], out_ref.at[:, pl.ds(start, part_cols)]).wait_recv()
     for copy in out_copies:
         copy.wait_send()
 
@@ -236,6 +255,7 @@
     chips = n_ctx // 2
     all_tokens = n_head * tokens
     rows = heads * all_tokens
+    parts = 2 if heads % 2 == 0 else 1
     bf16, f32 = jnp.bfloat16, jnp.float32
     dma = pltpu.SemaphoreType.DMA
     anywhere = pl.BlockSpec(memory_space=pltpu.HBM)
@@ -255,15 +275,15 @@
             pltpu.VMEM((chips, rows, 2 * span), f32),
             pltpu.VMEM((rows, LATENT), f32),
             pltpu.VMEM((all_tokens, heads * VDIM), f32),
-            pltpu.VMEM((n_head, tokens, heads * VDIM), bf16),
-            dma((6,)),
+            pltpu.VMEM((parts, n_head, tokens, heads // parts * VDIM), bf16),
+            dma((5 + parts,)),
             dma((n_head,)),
             dma((n_head,)),
             dma((chips,)),
             dma((chips,)),
             dma((chips, 2)),
-            dma((n_head,)),
-            dma((n_head,)),
+            dma((parts, n_head)),
+            dma((parts, n_head)),
         ],
         compiler_params=pltpu.CompilerParams(
             collective_id=0, has_side_effects=True, vmem_limit_bytes=64 * 1024 * 1024 - 64 * 1024

time: 20.1 us -> 20.4 us (1.015)
  Pallas kernels: 17.8 us -> 18.1 us
    pallas_call x1, Pallas kernels: 17.8 us -> 18.1 us  [local(): pl.pallas_call(functools.partial(kernel, n_head, n_ctx), out_shape=jax.Sh...]
where the time goes in v3:
time: 20.4 us; the launch traced here: 20.2 us
  Pallas kernels  18.1 us (89%)
  local copies, waits for them, and re-layouts  1.52 us (7%)
  between operations  0.66 us (3%)
    pallas_call x1, Pallas kernels, local(): pl.pallas_call(functools.partial(kernel, n_head, n_ctx), out_shape=jax.Sh...  18.1 us
    unnamed x1, local copies, waits for them, and re-layouts  1.52 us

profile of v3, /device:TPU:0, one launch (start us, length us, event | category | flops | bytes accessed | tf_op | source)
XLA Modules:
  0.0 20.2 jit_solution(8952244112727653275)
XLA Ops:
  0.7 18.1 %shard_map.55 = bf16[2,16384]{1,0:T(2,128)(2,1)} custom-call(bf16[2,24576]{1,0:T(2,128)(2,1)} %q_hbm.1, bf16[16,128,512]{2,1,0:T(8,128)(2,1)} %uk_hbm.1, bf16[16,512,128]{2,1,0:T(8,128)(2,1)} %uv_hbm.1, bf16[576,128]{1,0:T(8,128)(2,1)} %bitcast.1, s32[1]{0:T(128)S(6)} %copy.7.offset_ref), custom_call_target="tpu_custom_call" | custom-call | tf_op jit(solution)/shard_map/pallas_call | solution.py:262
  18.7 1.5 %copy.8 = bf16[2,16384]{1,0:T(2,128)(2,1)} copy(bf16[2,16384]{1,0:T(2,128)(2,1)} %shard_map.55) | data formatting | bytes 131072

commit v4 on v2

--- a/solution.py
+++ b/solution.py
@@ -238,12 +238,12 @@
     rows = heads * all_tokens
     bf16, f32 = jnp.bfloat16, jnp.float32
     dma = pltpu.SemaphoreType.DMA
-    anywhere = pl.BlockSpec(memory_space=pltpu.HBM)
+    anywhere = pl.BlockSpec(memory_space=pl.ANY)
     return pl.pallas_call(
         functools.partial(kernel, n_head, n_ctx),
         out_shape=jax.ShapeDtypeStruct((tokens, n_head * heads * VDIM), bf16),
         in_specs=[anywhere] * 4 + [pl.BlockSpec(memory_space=pltpu.SMEM)],
-        out_specs=pl.BlockSpec(memory_space=pltpu.VMEM),
+        out_specs=anywhere,
         scratch_shapes=[
             pltpu.VMEM(queries.shape, bf16),
             pltpu.VMEM((n_head, tokens, heads * WIDTH), bf16),

time: 20.1 us -> 19.6 us (0.975)
  Pallas kernels: 17.8 us -> 17.3 us
    pallas_call x1, Pallas kernels: 17.8 us -> 17.3 us  [local(): pl.pallas_call(functools.partial(kernel, n_head, n_ctx), out_shape=jax.Sh...]
where the time goes in v4:
time: 19.6 us; the launch traced here: 19.4 us
  Pallas kernels  17.3 us (88%)
  local copies, waits for them, and re-layouts  1.52 us (8%)
  between operations  0.66 us (3%)
    pallas_call x1, Pallas kernels, local(): pl.pallas_call(functools.partial(kernel, n_head, n_ctx), out_shape=jax.Sh...  17.3 us
    unnamed x1, local copies, waits for them, and re-layouts  1.52 us

profile of v4, /device:TPU:0, one launch (start us, length us, event | category | flops | bytes accessed | tf_op | source)
XLA Modules:
  0.0 19.4 jit_solution(14360774315311515877)
XLA Ops:
  0.7 17.3 %shard_map.55 = bf16[2,16384]{1,0:T(2,128)(2,1)} custom-call(bf16[2,24576]{1,0:T(2,128)(2,1)} %q_hbm.1, bf16[16,128,512]{2,1,0:T(8,128)(2,1)} %uk_hbm.1, bf16[16,512,128]{2,1,0:T(8,128)(2,1)} %uv_hbm.1, bf16[576,128]{1,0:T(8,128)(2,1)} %bitcast.1, s32[1]{0:T(128)S(6)} %copy.7.offset_ref), custom_call_target="tpu_custom_call" | custom-call | tf_op jit(solution)/shard_map/pallas_call | solution.py:242
  17.9 1.5 %copy.8 = bf16[2,16384]{1,0:T(2,128)(2,1)} copy(bf16[2,16384]{1,0:T(2,128)(2,1)} %shard_map.55) | data formatting | bytes 131072

commit v5 on v4

--- a/solution.py
+++ b/solution.py
@@ -53,8 +53,6 @@
     load_uv = pltpu.make_async_copy(uv_hbm, uv, local_sem.at[3])
     load_q.start()
     load_cache.start()
-    load_uk.start()
-    load_uv.start()
 
     barrier = pltpu.get_barrier_semaphore()
     for i in range(1, n_head):
@@ -65,9 +63,24 @@
         )
     pl.semaphore_signal(barrier, inc=1, device_id=(h_me, sibling), device_id_type=MESH)
     load_q.wait()
+    load_uk.start()
+    load_uv.start()
+    pl.semaphore_wait(barrier, n_head - 1 + chips)
+
+    q_copies = []
+    for i in range(1, n_head):
+        there = head_peer(i)
+        copy = pltpu.make_async_remote_copy(
+            src_ref=q_in.at[:, pl.ds(pl.multiple_of(there * q_cols, 128), q_cols)],
+            dst_ref=q_got.at[h_me],
+            send_sem=q_send.at[i],
+            recv_sem=q_recv.at[h_me],
+            device_id=(there, c_me),
+            device_id_type=MESH,
+        )
+        copy.start()
+        q_copies.append(copy)
     load_cache.wait()
-    pl.semaphore_wait(barrier, n_head - 1 + chips)
-
     cache_far = []
     for i in range(1, chips):
         there = chip_peer(i)
@@ -81,19 +94,6 @@
         )
         copy.start()
         cache_far.append(copy)
-    q_copies = []
-    for i in range(1, n_head):
-        there = head_peer(i)
-        copy = pltpu.make_async_remote_copy(
-            src_ref=q_in.at[:, pl.ds(pl.multiple_of(there * q_cols, 128), q_cols)],
-            dst_ref=q_got.at[h_me],
-            send_sem=q_send.at[i],
-            recv_sem=q_recv.at[h_me],
-            device_id=(there, c_me),
-            device_id_type=MESH,
-        )
-        copy.start()
-        q_copies.append(copy)
     to_sibling = pltpu.make_async_remote_copy(
         src_ref=piece(chip, core),
         dst_ref=piece(chip, core),

time: 19.6 us -> 19.6 us (level)
  no operation moved by 1% of the time
where the time goes in v5:
time: 19.6 us; the launch traced here: 19.4 us
  Pallas kernels  17.3 us (88%)
  local copies, waits for them, and re-layouts  1.52 us (8%)
  between operations  0.66 us (3%)
    pallas_call x1, Pallas kernels, local(): pl.pallas_call(functools.partial(kernel, n_head, n_ctx), out_shape=jax.Sh...  17.3 us
    unnamed x1, local copies, waits for them, and re-layouts  1.52 us

profile of v5, /device:TPU:0, one launch (start us, length us, event | category | flops | bytes accessed | tf_op | source)
XLA Modules:
  0.0 19.4 jit_solution(16006191638685580072)
XLA Ops:
  0.7 17.3 %shard_map.55 = bf16[2,16384]{1,0:T(2,128)(2,1)} custom-call(bf16[2,24576]{1,0:T(2,128)(2,1)} %q_hbm.1, bf16[16,128,512]{2,1,0:T(8,128)(2,1)} %uk_hbm.1, bf16[16,512,128]{2,1,0:T(8,128)(2,1)} %uv_hbm.1, bf16[576,128]{1,0:T(8,128)(2,1)} %bitcast.1, s32[1]{0:T(128)S(6)} %copy.7.offset_ref), custom_call_target="tpu_custom_call" | custom-call | tf_op jit(solution)/shard_map/pallas_call | solution.py:242
  17.9 1.5 %copy.8 = bf16[2,16384]{1,0:T(2,128)(2,1)} copy(bf16[2,16384]{1,0:T(2,128)(2,1)} %shard_map.55) | data formatting | bytes 131072

commit v6 on v5

--- a/solution.py
+++ b/solution.py
@@ -38,6 +38,8 @@
     core = c_me % 2
     sibling = chip * 2 + 1 - core
 
+    far_first = sorted(range(1, n_head), key=lambda i: abs(2 * i - n_head))
+
     def head_peer(i):
         return lax.rem(h_me + i, n_head)
 
@@ -68,7 +70,7 @@
     pl.semaphore_wait(barrier, n_head - 1 + chips)
 
     q_copies = []
-    for i in range(1, n_head):
+    for i in far_first:
         there = head_peer(i)
         copy = pltpu.make_async_remote_copy(
             src_ref=q_in.at[:, pl.ds(pl.multiple_of(there * q_cols, 128), q_cols)],
@@ -203,7 +205,7 @@
 
     mine = pl.ds(pl.multiple_of(h_me * o_cols, 128), o_cols)
     out_copies = []
-    for i in range(1, n_head):
+    for i in far_first:
         there = head_peer(i)
         copy = pltpu.make_async_remote_copy(
             src_ref=slabs.at[there],

time: 19.6 us -> 20.4 us (1.041)
  Pallas kernels: 17.3 us -> 18 us
    pallas_call x1, Pallas kernels: 17.3 us -> 18 us  [local(): pl.pallas_call(functools.partial(kernel, n_head, n_ctx), out_shape=jax.Sh...]
where the time goes in v6:
time: 20.4 us; the launch traced here: 20.2 us
  Pallas kernels  18 us (88%)
  local copies, waits for them, and re-layouts  1.52 us (7%)
  between operations  0.66 us (3%)
    pallas_call x1, Pallas kernels, local(): pl.pallas_call(functools.partial(kernel, n_head, n_ctx), out_shape=jax.Sh...  18 us
    unnamed x1, local copies, waits for them, and re-layouts  1.52 us

profile of v6, /device:TPU:0, one launch (start us, length us, event | category | flops | bytes accessed | tf_op | source)
XLA Modules:
  0.0 20.2 jit_solution(5631231791526970177)
XLA Ops:
  0.7 18.0 %shard_map.55 = bf16[2,16384]{1,0:T(2,128)(2,1)} custom-call(bf16[2,24576]{1,0:T(2,128)(2,1)} %q_hbm.1, bf16[16,128,512]{2,1,0:T(8,128)(2,1)} %uk_hbm.1, bf16[16,512,128]{2,1,0:T(8,128)(2,1)} %uv_hbm.1, bf16[576,128]{1,0:T(8,128)(2,1)} %bitcast.1, s32[1]{0:T(128)S(6)} %copy.7.offset_ref), custom_call_target="tpu_custom_call" | custom-call | tf_op jit(solution)/shard_map/pallas_call | solution.py:244
  18.7 1.5 %copy.8 = bf16[2,16384]{1,0:T(2,128)(2,1)} copy(bf16[2,16384]{1,0:T(2,128)(2,1)} %shard_map.55) | data formatting | bytes 131072

commit v7 on v5

--- a/solution.py
+++ b/solution.py
@@ -127,7 +127,7 @@
     for p in range(n_head):
         q_rows[p * tokens : (p + 1) * tokens, :] = q_got[p].astype(jnp.float32)
     load_uk.wait()
-    for pair in range(heads // 2):
+    def to_latent(pair):
         both = q_rows[:, pair * 2 * WIDTH : (pair + 1) * 2 * WIDTH].astype(jnp.bfloat16)
         for k in range(2):
             h = pair * 2 + k
@@ -139,6 +139,10 @@
             ).astype(jnp.bfloat16)
             q_all[at, LATENT:] = turned
 
+    pairs = heads // 2
+    for pair in range(pairs // 2):
+        to_latent(pair)
+
     forwards = []
     for i in range(1, chips):
         there = chip_peer(i)
@@ -153,6 +157,9 @@
         )
         copy.start()
         forwards.append(copy)
+
+    for pair in range(pairs // 2, pairs):
+        to_latent(pair)
 
     row = lax.broadcasted_iota(jnp.int32, (rows, 1), 0)
     token = lax.rem(row, all_tokens)

time: 19.6 us -> 19.9 us (1.015)
  Pallas kernels: 17.3 us -> 17.5 us
    pallas_call x1, Pallas kernels: 17.3 us -> 17.5 us  [local(): pl.pallas_call(functools.partial(kernel, n_head, n_ctx), out_shape=jax.Sh...]
where the time goes in v7:
time: 19.9 us; the launch traced here: 19.7 us
  Pallas kernels  17.5 us (88%)
  local copies, waits for them, and re-layouts  1.52 us (8%)
  between operations  0.66 us (3%)
    pallas_call x1, Pallas kernels, local(): pl.pallas_call(functools.partial(kernel, n_head, n_ctx), out_shape=jax.Sh...  17.5 us
    unnamed x1, local copies, waits for them, and re-layouts  1.52 us

profile of v7, /device:TPU:0, one launch (start us, length us, event | category | flops | bytes accessed | tf_op | source)
XLA Modules:
  0.0 19.7 jit_solution(14321203537715211026)
XLA Ops:
  0.7 17.5 %shard_map.55 = bf16[2,16384]{1,0:T(2,128)(2,1)} custom-call(bf16[2,24576]{1,0:T(2,128)(2,1)} %q_hbm.1, bf16[16,128,512]{2,1,0:T(8,128)(2,1)} %uk_hbm.1, bf16[16,512,128]{2,1,0:T(8,128)(2,1)} %uv_hbm.1, bf16[576,128]{1,0:T(8,128)(2,1)} %bitcast.1, s32[1]{0:T(128)S(6)} %copy.7.offset_ref), custom_call_target="tpu_custom_call" | custom-call | tf_op jit(solution)/shard_map/pallas_call | solution.py:249
  18.2 1.5 %copy.8 = bf16[2,16384]{1,0:T(2,128)(2,1)} copy(bf16[2,16384]{1,0:T(2,128)(2,1)} %shard_map.55) | data formatting | bytes 131072
